TPU v7x, 768 devices: a whole 4x8x12 slice. The times are simulated.
768 devices in a mesh: row: 16 (over x_hi, y), rep: 48 (over z, x_lo, core).
Axes of the slice: x: 4 (x_hi: 2, x_lo: 2; x = x_hi * 2 + x_lo), y: 8, z: 12, core: 2. Of those that a mesh axis runs over, the one named last changes fastest.
Arguments:
- node_features: bfloat16 [196608, 128], P(('row', 'rep')), may hold values from -6 to 6
- layer_weight: bfloat16 [128, 256], replicated, may hold values from -0.5 to 0.5
- tile_values: bfloat16 [16, 768, 8, 128, 128], P('row', 'rep'), may hold values from -0.078125 to 0.078125
- tile_positions: int32 [16, 768, 8], P('row', 'rep'), may hold values from 0 to 191, as said below
- section_tile_count: int32 [16, 768], P('row', 'rep'), may hold values from 1 to 8, as said below
- out_cotangent: bfloat16 [196608, 256], P(('row', 'rep')), may hold values from -0.019897461 to 0.019897461
Outputs:
- mixed_out: bfloat16 [196608, 256], P(('row', 'rep'))
- summed_grad: float32 [128, 256], replicated
Inputs may be any that keep to these rules, and one draw needn't show every extreme that they name: `tile_positions`: within one slab, replica and section the live codes are distinct; a code p names tile row p // 2 of the slab's 48 * 2 tile rows and tile column p % 2 of the section's node block. `section_tile_count`: every device (one slab and replica) has one section with all 8 slots live.
All inputs are finite; a program needn't handle non-finite values.
Results may differ from a plain program's by a relative error of at most 0.0049.
Values may be sent and summed in bfloat16 or wider, within the bound.
A program may use at most 32 MiB of HBM per device.

v0:
```python
import jax
import jax.numpy as jnp
from jax import lax
from jax.sharding import PartitionSpec as P


def section_add(
    partial_value, section_block, section_index, tile_values, tile_positions, section_tile_count
):
    tile_edge = tile_values.shape[-1]
    feature_width = section_block.shape[-1]
    blocks_held = section_block.shape[0] // tile_edge
    adjacency_values = lax.dynamic_index_in_dim(tile_values, section_index, 0, keepdims=False)
    placed = lax.dynamic_index_in_dim(tile_positions, section_index, 0, keepdims=False)
    live_count = lax.dynamic_index_in_dim(section_tile_count, section_index, 0, keepdims=False)
    tile_row = placed // blocks_held
    tile_col = placed % blocks_held
    selected_tiles = section_block.reshape(blocks_held, tile_edge, feature_width)[tile_col]
    tile_products = jnp.einsum(
        "nqi,nir->nqr", adjacency_values, selected_tiles, preferred_element_type=jnp.float32
    )
    living = jnp.arange(adjacency_values.shape[0], dtype=jnp.int32) < live_count
    tile_products = jnp.where(living[:, None, None], tile_products, 0.0)
    shaped = partial_value.reshape(-1, tile_edge, feature_width)
    return shaped.at[tile_row].add(tile_products).reshape(partial_value.shape)


def body(
    node_features, layer_weight, tile_values, tile_positions, section_tile_count, out_cotangent
):
    local_tiles = tile_values[0]
    local_positions = tile_positions[0]
    local_counts = section_tile_count[0]
    rows_held = node_features.shape[0]
    sections = lax.axis_size("row")
    cleared_output = jnp.zeros(
        (rows_held * lax.axis_size("rep"), node_features.shape[1]), jnp.float32
    )
    collected_rows = lax.all_gather(node_features, "row", axis=0, tiled=True)

    def through_all(offset, carried_state):
        section_block = lax.dynamic_slice_in_dim(collected_rows, offset * rows_held, rows_held, 0)
        return section_add(
            carried_state, section_block, offset, local_tiles, local_positions, local_counts
        )

    partial_value = lax.fori_loop(0, sections, through_all, cleared_output)
    aggregate = lax.psum_scatter(partial_value, "rep", scatter_dimension=0, tiled=True)
    mixed_out = jnp.dot(
        aggregate.astype(jnp.bfloat16), layer_weight, preferred_element_type=jnp.float32
    ).astype(jnp.bfloat16)
    local_grad = jnp.einsum(
        "nf,nh->fh", aggregate, out_cotangent.astype(jnp.float32), precision=lax.Precision.HIGHEST
    )
    summed_grad = lax.psum(local_grad, ("row", "rep"))
    return (mixed_out, summed_grad)


def solution(mesh):
    placed = (
        P(("row", "rep"), None),
        P(),
        P("row", "rep", None, None, None),
        P("row", "rep", None),
        P("row", "rep"),
        P(("row", "rep"), None),
    )
    return jax.shard_map(
        body, mesh=mesh, in_specs=placed, out_specs=(P(("row", "rep"), None), P()), check_vma=False
    )
```

profile of v0, /device:TPU:1, one launch (start us, length us, event | category | flops | bytes accessed | tf_op | source)
XLA Modules:
  0.0 867.6 jit_solution(12182929573983667736)
XLA Ops:
  8.7 96.4 %all-gather.2.cloned.1.call-done = bf16[4096,128]{1,0:T(8,128)(2,1)} async-done(((bf16[256,128]{1,0:T(8,128)(2,1)}), bf16[4096,128]{1,0:T(8,128)(2,1)}) %all-gather.2.cloned.1.call-update) | async-done | bytes 1048592 | tf_op jit(solution)/shard_map/all_gather | solution.py:39
  105.2 2.9 broadcast_in_dim.45
  108.0 106.2 %while.15 = (s32[]{:T(128)}, f32[12288,128]{1,0:T(8,128)}, s32[16,8]{1,0:T(8,128)S(1)}, s32[16]{0:T(128)S(1)}, bf16[16,8,128,128]{3,2,1,0:T(8,128)(2,1)}, /*inde...) while((s32[]{:T(128)}, f32[12288,128]{1,0:T(8,128)}, s32[16,8]{1,0:T(8,128)S(1)}, ...), condition=%wide.region_2.3_spmd, body=%wide.region_0.2_spmd.sunk | while | flops 33817844 | bytes 3281387 | solution.py:47
  109.3 0.9 constant_dynamic-slice_fusion.3
  110.8 1.2 convolution_select_fusion.2
  112.0 2.7 scatter_fusion
  116.0 0.9 constant_dynamic-slice_fusion.3
  117.4 1.2 convolution_select_fusion.2
  118.6 2.7 scatter_fusion
  122.6 0.9 constant_dynamic-slice_fusion.3
  124.0 1.2 convolution_select_fusion.2
  125.2 2.7 scatter_fusion
  129.2 0.9 constant_dynamic-slice_fusion.3
  130.7 1.2 convolution_select_fusion.2
  131.8 2.7 scatter_fusion
  135.9 0.9 constant_dynamic-slice_fusion.3
  137.3 1.2 convolution_select_fusion.2
  138.5 2.7 scatter_fusion
  142.5 0.9 constant_dynamic-slice_fusion.3
  143.9 1.2 convolution_select_fusion.2
  145.1 2.7 scatter_fusion
  149.2 0.9 constant_dynamic-slice_fusion.3
  150.6 1.2 convolution_select_fusion.2
  151.8 2.7 scatter_fusion
  155.8 0.9 constant_dynamic-slice_fusion.3
  157.3 1.2 convolution_select_fusion.2
  158.4 2.7 scatter_fusion
  163.9 1.2 convolution_select_fusion.2
  165.1 2.7 scatter_fusion
  170.5 1.2 convolution_select_fusion.2
  171.7 2.7 scatter_fusion
  177.1 1.2 convolution_select_fusion.2
  178.3 2.7 scatter_fusion
  183.8 1.2 convolution_select_fusion.2
  184.9 2.7 scatter_fusion
  190.4 1.2 convolution_select_fusion.2
  191.6 2.7 scatter_fusion
  197.0 1.2 convolution_select_fusion.2
  198.2 2.7 scatter_fusion
  203.7 1.2 convolution_select_fusion.2
  204.9 2.7 scatter_fusion
  210.3 1.2 convolution_select_fusion.2
  211.5 2.7 scatter_fusion
  214.3 183.2 %reduce-scatter.2.cloned.1.call-done = f32[256,128]{1,0:T(8,128)} async-done(((f32[12288,128]{1,0:T(8,128)}), f32[256,128]{1,0:T(8,128)}) %reduce-scatter.2.cloned.1.call-update) | async-done | bytes 131088 | tf_op jit(solution)/shard_map/reduce_scatter | solution.py:48
  397.4 1.8 fusion.7
  399.3 1.7 convolution_convert_fusion
  401.0 458.5 %all-reduce.2.cloned.1.call-done = f32[128,256]{1,0:T(8,128)} async-done(((f32[128,256]{1,0:T(8,128)}), f32[128,256]{1,0:T(8,128)}) %all-reduce.2.cloned.1.call-update) | async-done | bytes 131088 | tf_op jit(solution)/shard_map/psum | solution.py:55
  859.6 1.6 copy.17
  (117 shorter events, 38.4 us)
Async XLA Ops:
  7.2 390.3 %copy-start = (bf16[256,256]{1,0:T(8,128)(2,1)S(1)}, bf16[256,256]{1,0:T(8,128)(2,1)}, u32[]{:S(2)}) copy-start(bf16[256,256]{1,0:T(8,128)(2,1)} %param.13) | copy-start | bytes 393220
  7.2 100.8 %copy-start.2 = (s32[1,16]{1,0:T(1,128)S(1)}, s32[1,16]{1,0:T(1,128)}, u32[]{:S(2)}) copy-start(s32[1,16]{1,0:T(1,128)} %param.12) | copy-start | bytes 196
  7.2 98.0 %all-gather.2.cloned.1.call-start = ((), (), s32[]{:S(2)}) async-start(), calls=%async_computation.1 | async-start | bytes 1114112 | tf_op jit(solution)/shard_map/all_gather | solution.py:39
  7.9 389.5 %reduce-scatter.2.cloned.1.call-start = ((), (), s32[]{:S(2)}) async-start(), calls=%async_computation.2 | async-start | bytes 6422528 | tf_op jit(solution)/shard_map/reduce_scatter | solution.py:48
  214.2 185.1 %copy-start.1 = (bf16[128,256]{1,0:T(8,128)(2,1)S(1)}, bf16[128,256]{1,0:T(8,128)(2,1)}, u32[]{:S(2)}) copy-start(bf16[128,256]{1,0:T(8,128)(2,1)} %param.9) | copy-start | bytes 196612
  214.2 645.3 %all-reduce.2.cloned.1.call-start = ((), (), s32[]{:S(2)}) async-start(), calls=%async_computation.3 | async-start | bytes 262144 | tf_op jit(solution)/shard_map/psum | solution.py:55
Sparse Core Ops, SparseCore 0:
  11.8 93.3 all-gather.1
  214.3 183.0 reduce-scatter.1
  403.4 456.0 all-reduce.1
where the time goes:
time: 871 us; the launch traced here: 868 us
  waiting for transfers between devices  739 us (85%)
  other arithmetic  54.3 us (6%)
  local copies, waits for them, and re-layouts  37.7 us (4%)
  matrix products  22.3 us (3%)
  between operations  13.8 us (2%)
    psum x1, waiting for transfers between devices, body(): summed_grad = lax.psum(local_grad, ('row', 'rep'))  459 us
    reduce_scatter x1, waiting for transfers between devices, body(): lax.psum_scatter(partial_value, 'rep', scatter_dimension=0, tiled=True)  183 us
    all_gather x1, waiting for transfers between devices, body(): collected_rows = lax.all_gather(node_features, 'row', axis=0, tiled=True)  96.4 us
    scatter-add x16, other arithmetic, section_add(): return shaped.at[tile_row].add(tile_products).reshape(partial_value.shape)  43.2 us
    dot_general x16, matrix products, section_add(): jnp.einsum('nqi,nir->nqr', adjacency_values, selected_tiles, preferred_el...  18.7 us
  transfers between devices with their start and end apart: 3, of which 3 were waited for; matrix products, arithmetic and copies ran while one was open for 0% of the time, Pallas kernels for 0%

commit v1 on v0

v1 whole, which is shorter than its diff:
```python
import functools

import jax
import jax.numpy as jnp
from jax import lax
from jax.experimental import pallas as pl
from jax.experimental.pallas import tpu as pltpu
from jax.sharding import PartitionSpec as P

MESH = pl.DeviceIdType.MESH
F32, BF16 = jnp.float32, jnp.bfloat16
XH, XL, CORES = 2, 2, 2


def place(ny):
    row, rep = lax.axis_index("row"), lax.axis_index("rep")
    return row // ny, lax.rem(row, ny), rep // 4, lax.rem(rep // 2, 2), lax.rem(rep, 2)


def greet(peers):
    barrier = pltpu.get_barrier_semaphore()
    for peer in peers:
        pl.semaphore_signal(barrier, inc=1, device_id=peer, device_id_type=MESH)
    pl.semaphore_wait(barrier, len(peers))


def gather_kernel(ny, x_ref, out_ref, send_sem, recv_sem, own_sem):
    xh, y, z, xl, c = place(ny)
    row, rep = lax.axis_index("row"), lax.axis_index("rep")
    half = ny // 2
    partner = ((1 - xh) * ny + y, rep)
    up = (xh * ny + lax.rem(y + 1, ny), rep)
    down = (xh * ny + lax.rem(y + ny - 1, ny), rep)
    greet([partner] + ([up, down] if ny > 2 else [up]))
    own = pltpu.make_async_copy(x_ref, out_ref.at[row], own_sem)
    own.start()
    started = []

    def send(src, slot, peer, k):
        copy = pltpu.make_async_remote_copy(
            src, out_ref.at[slot], send_sem.at[k], recv_sem.at[k], device_id=peer, device_id_type=MESH
        )
        copy.start()
        started.append(copy)
        return copy

    def slot_of(side, shift):
        return side * ny + lax.rem(y + shift + ny, ny)

    count = 1
    flows = [(0, 1, half), (0, -1, half - 1), (1, 1, half - 1), (1, -1, half)]
    last = [None] * 4
    cross = None
    for step in range(half):
        for f, (side, way, steps) in enumerate(flows):
            if step >= steps:
                continue
            which = xh if side == 0 else 1 - xh
            slot = slot_of(which, -way * step)
            src = out_ref.at[slot]
            if step == 0:
                if side == 0:
                    src = x_ref
                elif cross is not None and last[2] is None and last[3] is None:
                    cross.wait_recv()
            else:
                last[f].wait_recv()
            last[f] = send(src, slot, up if way == 1 else down, count)
            count += 1
            if step == 0 and f == 0:
                cross = send(x_ref, row, partner, 0)
    if ny == 2:
        pass
    own.wait()
    for f in range(4):
        if last[f] is not None:
            last[f].wait_recv()
    for copy in started:
        copy.wait_send()


def gather(x, ny):
    copies = 1 + 2 * (ny - 1)
    return pl.pallas_call(
        functools.partial(gather_kernel, ny),
        out_shape=jax.ShapeDtypeStruct((XH * ny,) + x.shape, x.dtype),
        in_specs=[pl.BlockSpec(memory_space=pltpu.VMEM)],
        out_specs=pl.BlockSpec(memory_space=pltpu.VMEM),
        scratch_shapes=[
            pltpu.SemaphoreType.DMA((copies,)),
            pltpu.SemaphoreType.DMA((copies,)),
            pltpu.SemaphoreType.DMA,
        ],
        compiler_params=pltpu.CompilerParams(
            collective_id=0, has_side_effects=True, vmem_limit_bytes=16 << 20
        ),
        name="gather_features",
    )(x)


def section_kernel(tiles_all, pos_ref, cnt_ref, tile_ref, x_ref, own_ref, oth_ref, acc, prod):
    j = pl.program_id(0)
    sections = pl.num_programs(0)
    cap, edge = tile_ref.shape[1], tile_ref.shape[2]
    core = lax.rem(lax.axis_index("rep"), 2)
    half = tiles_all // 2

    @pl.when(j == 0)
    def _():
        def clear(t, carry):
            acc[t] = jnp.zeros(acc.shape[1:], F32)
            return carry

        lax.fori_loop(0, tiles_all, clear, 0)

    both = jnp.concatenate([x_ref[j, :edge], x_ref[j, edge:]], axis=1)
    tiles = tile_ref[0].reshape(cap * edge, edge)
    prod[...] = jnp.dot(tiles, both, preferred_element_type=F32)
    live = cnt_ref[j]
    for s in range(cap):
        p = pos_ref[j, s]
        t = p // 2
        chunk = t // 2
        spot = jnp.where(lax.rem(chunk, 2) == core, 0, half) + (chunk // 2) * 2 + lax.rem(t, 2)
        spot = jnp.where(s < live, spot, tiles_all)
        lane = pl.multiple_of(lax.rem(p, 2) * edge, edge)
        acc[spot] += prod[s * edge : (s + 1) * edge, pl.ds(lane, edge)]

    @pl.when(j == sections - 1)
    def _():
        def out(k, carry):
            own_ref[k] = acc[k]
            oth_ref[k] = acc[half + k].astype(BF16)
            return carry

        lax.fori_loop(0, half, out, 0)


def section_sums(tiles, positions, counts, rows, reps):
    sections, cap, edge, _ = tiles.shape
    tiles_all = reps * 2
    return pl.pallas_call(
        functools.partial(section_kernel, tiles_all),
        out_shape=(
            jax.ShapeDtypeStruct((tiles_all // 2, edge, edge), F32),
            jax.ShapeDtypeStruct((tiles_all // 2, edge, edge), BF16),
        ),
        grid_spec=pltpu.PrefetchScalarGridSpec(
            num_scalar_prefetch=2,
            grid=(sections,),
            in_specs=[
                pl.BlockSpec((1, cap, edge, edge), lambda j, *_: (j, 0, 0, 0)),
                pl.BlockSpec(rows.shape, lambda j, *_: (0, 0, 0)),
            ],
            out_specs=(
                pl.BlockSpec((tiles_all // 2, edge, edge), lambda j, *_: (0, 0, 0)),
                pl.BlockSpec((tiles_all // 2, edge, edge), lambda j, *_: (0, 0, 0)),
            ),
            scratch_shapes=[
                pltpu.VMEM((tiles_all + 1, edge, edge), F32),
                pltpu.VMEM((cap * edge, 2 * edge), F32),
            ],
        ),
        compiler_params=pltpu.CompilerParams(vmem_limit_bytes=40 << 20),
        name="section_products",
    )(positions, counts, tiles, rows)


def reduce_kernel(
    ny, nz, own_ref, oth_ref, w_ref, g_ref, mixed_ref, grad_ref,
    cbuf, sbuf, rbuf, xsend, xrecv, gbuf, r1, hbuf, r2, vbuf, r3, ubuf, r4, tbuf, r5, r6,
    c_s, c_r, z_s, z_r, x_s, x_r, a_s, a_r,
):
    xh, y, z, xl, c = place(ny)
    row, rep = lax.axis_index("row"), lax.axis_index("rep")
    half = nz // 2
    core_peer = (row, rep + 1 - 2 * c)
    x_peer = (row, z * 4 + (1 - xl) * 2 + c)

    def z_peer(d):
        return (row, lax.rem(z + d + nz, nz) * 4 + xl * 2 + c)

    def y_peer(d):
        return (xh * ny + lax.rem(y + d, ny), rep)

    x = xh * 2 + xl

    def x4_peer(d):
        q = lax.rem(x + d, 4)
        return ((q // 2) * ny + y, z * 4 + lax.rem(q, 2) * 2 + c)

    greet(
        [core_peer]
        + [z_peer(d) for d in range(1, nz)]
        + [y_peer(d) for d in range(1, ny)]
        + [x4_peer(d) for d in range(1, 4)]
    )
    started = []

    def send(src, dst, s_sem, r_sem, peer):
        copy = pltpu.make_async_remote_copy(src, dst, s_sem, r_sem, device_id=peer, device_id_type=MESH)
        copy.start()
        started.append(copy)
        return copy

    order = [half]
    for d in range(half - 1, 0, -1):
        order += [d, -d]
    order.append(0)
    cross = {}
    for k, d in enumerate(order):
        at = lax.rem(z + d + nz, nz)
        cross[d] = send(oth_ref.at[at], cbuf.at[at], c_s.at[k], c_r.at[k], core_peer)
    ready = set()

    def mine(d, side):
        if d == -half:
            d = half
        if d not in ready:
            cross[d].wait_recv()
            ready.add(d)
        at = lax.rem(z + d + nz, nz)
        return own_ref[at, side] + cbuf[at, side].astype(F32)

    side_a, side_b = 1 - xl, xl
    flows = [(0, 1, half), (0, -1, half - 1), (1, 1, half - 1), (1, -1, half)]
    last = [None] * 4
    count = 0
    for step in range(half):
        for f, (side, way, steps) in enumerate(flows):
            if step < half - steps:
                continue
            distance = half - step
            total = mine(way * distance, side_a if side == 0 else side_b)
            if last[f] is not None:
                last[f][0].wait_recv()
                total = total + rbuf[last[f][1]].astype(F32)
            sbuf[count] = total.astype(BF16)
            last[f] = (send(sbuf.at[count], rbuf.at[count], z_s.at[count], z_r.at[count], z_peer(way)), count)
            count += 1

    def finish(side, first, second):
        total = mine(0, side)
        for f in (first, second):
            if last[f] is not None:
                last[f][0].wait_recv()
                total = total + rbuf[last[f][1]].astype(F32)
        return total

    xsend[...] = finish(side_a, 0, 1)
    over = send(xsend, xrecv, x_s, x_r, x_peer)
    kept = finish(side_b, 2, 3)
    over.wait_recv()
    aggregate = kept + xrecv[...]
    gbuf[...] = lax.dot_general(
        aggregate, g_ref[...].astype(F32), (((0,), (0,)), ((), ())),
        precision=lax.Precision.HIGHEST, preferred_element_type=F32,
    )

    used = [0]

    def pair():
        k = used[0]
        used[0] += 1
        return a_s.at[k], a_r.at[k]

    hrows = gbuf.shape[0] // 2
    piece = hrows // ny
    first = send(gbuf.at[pl.ds(pl.multiple_of((1 - c) * hrows, hrows), hrows)], r1, *pair(), core_peer)
    mixed_ref[...] = jnp.dot(
        aggregate.astype(BF16), w_ref[...], preferred_element_type=F32
    ).astype(BF16)
    first.wait_recv()
    hbuf[...] = (gbuf[pl.ds(pl.multiple_of(c * hrows, hrows), hrows)] + r1[...]).reshape(hbuf.shape)

    def spread(src_of, slots, mine_at, peers):
        copies = []
        for k, peer in enumerate(peers):
            copies.append(send(src_of(k + 1), slots.at[mine_at], *pair(), peer))
        return copies

    def total_of(slots, n):
        total = slots[0]
        for k in range(1, n):
            total = total + slots[k]
        return total

    r2[y] = hbuf[y]
    for copy in spread(lambda d: hbuf.at[lax.rem(y + d, ny)], r2, y, [y_peer(d) for d in range(1, ny)]):
        copy.wait_recv()
    vbuf[...] = total_of(r2, ny)
    r3[x] = vbuf[...]
    for copy in spread(lambda d: vbuf, r3, x, [x4_peer(d) for d in range(1, 4)]):
        copy.wait_recv()
    ubuf[...] = total_of(r3, 4)
    r4[z] = ubuf[...]
    for copy in spread(lambda d: ubuf, r4, z, [z_peer(d) for d in range(1, nz)]):
        copy.wait_recv()
    tbuf[...] = total_of(r4, nz)
    r5[y] = tbuf[...]
    back = spread(lambda d: tbuf, r5, y, [y_peer(d) for d in range(1, ny)])
    other = [send(tbuf, r6.at[y], *pair(), core_peer)]
    for d, copy in enumerate(back):
        copy.wait_recv()
        at = lax.rem(y - (d + 1) + ny, ny)
        other.append(send(r5.at[at], r6.at[at], *pair(), core_peer))
    for copy in other:
        copy.wait_recv()
    grad_ref[pl.ds(pl.multiple_of(c * hrows, hrows), hrows)] = r5[...].reshape(hrows, -1)
    grad_ref[pl.ds(pl.multiple_of((1 - c) * hrows, hrows), hrows)] = r6[...].reshape(hrows, -1)
    for copy in started:
        copy.wait_send()


def reduce_all(own, oth, w, g, ny, nz):
    f, h = w.shape
    rows = g.shape[0]
    copies = nz - 1 + nz - 1
    hrows = f // 2
    piece = hrows // ny
    small = 1 + 2 * (ny - 1) + 3 + (nz - 1) + ny
    dma = pltpu.SemaphoreType.DMA
    return pl.pallas_call(
        functools.partial(reduce_kernel, ny, nz),
        out_shape=(
            jax.ShapeDtypeStruct((rows, h), BF16),
            jax.ShapeDtypeStruct((f, h), F32),
        ),
        in_specs=[pl.BlockSpec(memory_space=pltpu.VMEM)] * 4,
        out_specs=(pl.BlockSpec(memory_space=pltpu.VMEM),) * 2,
        scratch_shapes=[
            pltpu.VMEM((nz, 2, rows, f), BF16),
            pltpu.VMEM((copies, rows, f), BF16),
            pltpu.VMEM((copies, rows, f), BF16),
            pltpu.VMEM((rows, f), F32),
            pltpu.VMEM((rows, f), F32),
            pltpu.VMEM((f, h), F32),
            pltpu.VMEM((hrows, h), F32),
            pltpu.VMEM((ny, piece, h), F32),
            pltpu.VMEM((ny, piece, h), F32),
            pltpu.VMEM((piece, h), F32),
            pltpu.VMEM((4, piece, h), F32),
            pltpu.VMEM((piece, h), F32),
            pltpu.VMEM((nz, piece, h), F32),
            pltpu.VMEM((piece, h), F32),
            pltpu.VMEM((ny, piece, h), F32),
            pltpu.VMEM((ny, piece, h), F32),
            dma((nz,)), dma((nz,)), dma((copies,)), dma((copies,)), dma, dma, dma((small,)), dma((small,)),
        ],
        compiler_params=pltpu.CompilerParams(
            collective_id=1, has_side_effects=True, vmem_limit_bytes=40 << 20
        ),
        name="reduce_and_grad",
    )(own.reshape(nz, 2, rows, f), oth.reshape(nz, 2, rows, f), w, g)


def body(node_features, layer_weight, tile_values, tile_positions, section_tile_count, out_cotangent):
    ny = lax.axis_size("row") // XH
    reps = lax.axis_size("rep")
    nz = reps // (XL * CORES)
    rows = gather(node_features, ny)
    own, oth = section_sums(tile_values[0], tile_positions[0], section_tile_count[0], rows, reps)
    return reduce_all(own, oth, layer_weight, out_cotangent, ny, nz)


def solution(mesh):
    placed = (
        P(("row", "rep"), None),
        P(),
        P("row", "rep", None, None, None),
        P("row", "rep", None),
        P("row", "rep"),
        P(("row", "rep"), None),
    )
    return jax.shard_map(
        body, mesh=mesh, in_specs=placed, out_specs=(P(("row", "rep"), None), P()), check_vma=False
    )
```

time: 871 us -> 109 us (0.13)
  waiting for transfers between devices: 739 us -> 0 us
  Pallas kernels: 0 us -> 102 us
  other arithmetic: 54.3 us -> 0 us
  local copies, waits for them, and re-layouts: 37.7 us -> 5.76 us
  matrix products: 22.3 us -> 0 us
  between operations: 13.8 us -> 0.68 us
    psum x1 -> x0, waiting for transfers between devices: 459 us -> none  [body(): summed_grad = lax.psum(local_grad, ('row', 'rep'))]
    reduce_scatter x1 -> x0, waiting for transfers between devices: 183 us -> none  [body(): lax.psum_scatter(partial_value, 'rep', scatter_dimension=0, tiled=True)]
    pallas_call x0 -> x3, Pallas kernels: none -> 102 us  [the longest x1 73.1 us: reduce_all(): pl.pallas_call(functools.partial(reduce_kernel, ny, nz), out_shape=(jax.S...]
    all_gather x1 -> x0, waiting for transfers between devices: 96.4 us -> none  [body(): collected_rows = lax.all_gather(node_features, 'row', axis=0, tiled=True)]
    scatter-add x16 -> x0, other arithmetic: 43.2 us -> none  [section_add(): return shaped.at[tile_row].add(tile_products).reshape(partial_value.shape)]
    dynamic_slice x32 -> x0, local copies, waits for them, and re-layouts: 22.9 us -> none  [the longest x16 13.6 us: through_all(): lax.dynamic_slice_in_dim(collected_rows, offset * rows_held, rows_held, 0)]
    dot_general x18 -> x0, matrix products: 22.3 us -> none  [the longest x16 18.7 us: section_add(): jnp.einsum('nqi,nir->nqr', adjacency_values, selected_tiles, preferred_el...]
    lt x16 -> x0, other arithmetic: 10.4 us -> none  [section_add(): living = jnp.arange(adjacency_values.shape[0], dtype=jnp.int32) < live_count]
  transfers between devices with their start and end apart: 3 -> 0, of which waited for: 3 -> 0; matrix products, arithmetic and copies ran while one was open for 0% -> 0% of each run, Pallas kernels for 0% -> 0%
where the time goes in v1:
time: 109 us
  Pallas kernels  102 us (94%)
  local copies, waits for them, and re-layouts  5.76 us (5%)
    pallas_call x1, Pallas kernels, reduce_all(): pl.pallas_call(functools.partial(reduce_kernel, ny, nz), out_shape=(jax.S...  73.1 us
    pallas_call x1, Pallas kernels, gather(): pl.pallas_call(functools.partial(gather_kernel, ny), out_shape=jax.ShapeD...  20.8 us
    pallas_call x1, Pallas kernels, section_sums(): pl.pallas_call(functools.partial(section_kernel, tiles_all), out_shape=(j...  8.36 us
    unnamed x12, local copies, waits for them, and re-layouts  5 us

profile of v1, /device:TPU:1, one launch (start us, length us, event | category | flops | bytes accessed | tf_op | source)
XLA Modules:
  0.0 108.8 jit_solution(16711300213875781473)
XLA Ops:
  0.6 0.8 copy.8.pos_ref
  1.4 0.0 copy-start.3
  1.4 0.8 copy-done.3
  2.2 0.0 copy-start.1
  2.2 0.0 copy-start.2
  2.2 20.8 %gather_features.1.x_ref = bf16[16,256,128]{2,1,0:T(8,128)(2,1)S(1)} custom-call(bf16[256,128]{1,0:T(8,128)(2,1)S(1)} %copy-done.3), custom_call_target="tpu_custom_call" | custom-call | tf_op jit(solution)/shard_map/gather_features/pallas_call | solution.py:84
  23.1 0.0 copy-start
  23.1 2.2 %copy-done = bf16[1,16,8,128,128]{4,3,2,1,0:T(8,128)(2,1)S(1)} copy-done((bf16[1,16,8,128,128]{4,3,2,1,0:T(8,128)(2,1)S(1)}, bf16[1,16,8,128,128]{4,3,2,1,0:T(8,128)(2,1)}, u32[]{:S(2)}) %copy-start) | copy-done | bytes 4194328
  25.3 0.0 copy-start.4
  25.3 0.7 copy-done.4
  25.9 8.4 %section_products.1 = (f32[48,128,128]{2,1,0:T(8,128)S(1)}, bf16[48,128,128]{2,1,0:T(8,128)(2,1)S(1)}) custom-call(s32[16,8]{1,0:T(8,128)S(1)} %copy.8.pos_ref, s32[16]{0:T(128)S(1)} %bitcast.8, bf16[16,8,128,128]{3,2,1,0:T(8,128)(2,1)S(1)} %bitcast.5, bf16[16,256,128]{2,1,0:T(8,128)(2,1)S(1)} %gather_features.1.x_ref), custom_call_target="tpu_custom_call" | custom-call | tf_op jit(solution)/shard_map/section_products/pallas_call | solution.py:142
  34.3 0.0 copy-done.1
  34.3 0.0 copy-done.2
  34.3 73.1 %reduce_and_grad.1 = (bf16[256,256]{1,0:T(8,128)(2,1)S(1)}, f32[128,256]{1,0:T(8,128)S(1)}) custom-call(f32[12,2,256,128]{3,2,1,0:T(8,128)S(1)} %bitcast.6, bf16[12,2,256,128]{3,2,1,0:T(8,128)(2,1)S(1)} %bitcast.7, bf16[128,256]{1,0:T(8,128)(2,1)S(1)} %copy-done.2, bf16[256,256]{1,0:T(8,128)(2,1)S(1)} %copy-done.1), custom_call_target="tpu_custom_call" | custom-call | tf_op jit(solution)/shard_map/reduce_and_grad/pallas_call | solution.py:323
  107.4 0.7 copy.11
  108.1 0.7 copy.12
Async XLA Ops:
  1.4 0.8 copy-start.3
  2.2 32.1 %copy-start.1 = (bf16[256,256]{1,0:T(8,128)(2,1)S(1)}, bf16[256,256]{1,0:T(8,128)(2,1)}, u32[]{:S(2)}) copy-start(bf16[256,256]{1,0:T(8,128)(2,1)} %g_ref.1) | copy-start | bytes 393220
  2.2 32.1 %copy-start.2 = (bf16[128,256]{1,0:T(8,128)(2,1)S(1)}, bf16[128,256]{1,0:T(8,128)(2,1)}, u32[]{:S(2)}) copy-start(bf16[128,256]{1,0:T(8,128)(2,1)} %w_ref.1) | copy-start | bytes 196612
  23.1 2.2 %copy-start = (bf16[1,16,8,128,128]{4,3,2,1,0:T(8,128)(2,1)S(1)}, bf16[1,16,8,128,128]{4,3,2,1,0:T(8,128)(2,1)}, u32[]{:S(2)}) copy-start(bf16[1,16,8,128,128]{4,3,2,1,0:T(8,128)(2,1)} %param.8) | copy-start | bytes 12582916
  25.3 0.7 copy-start.4

commit v2 on v0

v2 whole, which is shorter than its diff:
```python
import functools

import jax
import jax.numpy as jnp
from jax import lax
from jax.experimental import pallas as pl
from jax.experimental.pallas import tpu as pltpu
from jax.sharding import PartitionSpec as P

MESH = pl.DeviceIdType.MESH
F32, BF16, I32 = jnp.float32, jnp.bfloat16, jnp.int32
XH, XL, CORES = 2, 2, 2
PIECES = 2


def iota(shape, dim):
    return lax.broadcasted_iota(I32, shape, dim)


def sort_slots(pos, cnt, tiles_all, width):
    n, cap = pos.shape
    slots = n * cap
    diag = iota((n, n), 0) == iota((n, n), 1)
    count = jnp.sum(jnp.where(diag, jnp.broadcast_to(cnt, (n, n)), 0), axis=1, keepdims=True)
    slot = iota((n, cap), 1)
    key = jnp.where(slot < count, lax.div(pos, 2), tiles_all)
    code = (key * slots + iota((n, cap), 0) * cap + slot) * 2 + lax.rem(pos, 2)
    spread = jnp.broadcast_to(code[:, None, :], (n, cap, cap))
    picked = jnp.where(iota((n, cap, cap), 1) == iota((n, cap, cap), 2), spread, 0)
    column = jnp.sum(picked, axis=2, keepdims=True).reshape(slots, 1)
    grid = jnp.broadcast_to(column, (slots, slots))
    lane = iota((slots, slots), 1)
    line = jnp.sum(jnp.where(iota((slots, slots), 0) == lane, grid, 0), axis=0, keepdims=True)
    rank = jnp.sum(jnp.where(line < grid, 1, 0), axis=1, keepdims=True)
    ordered = jnp.sum(jnp.where(rank == lane, grid, 0), axis=0, keepdims=True)
    rows = lax.div(jnp.broadcast_to(column, (slots, width)), 2 * slots)
    ends = jnp.sum(jnp.where(rows <= iota((slots, width), 1), 1, 0), axis=0, keepdims=True)
    return ordered, ends


def kernel(
    ny, nz, reach, x_ref, w_ref, tile_ref, pos_ref, cnt_ref, g_ref, mixed_ref, grad_ref,
    tiles, xall, prod, runs, codes_v, ends_v, codes, ends, gall, oth, cbuf, sbuf, rbuf, mbuf,
    xsend, xrecv, gbuf, r1, hbuf, r2, vbuf, r3, ubuf, r4, tbuf, r5, r6,
    t_s, i_s, ag_s, ag_r, g_s, g_r, c_s, c_r, z_s, z_r, x_s, x_r, a_s, a_r,
):
    row, rep = lax.axis_index("row"), lax.axis_index("rep")
    xh, y = row // ny, lax.rem(row, ny)
    z, xl, c = rep // 4, lax.rem(rep // 2, 2), lax.rem(rep, 2)
    x = xh * 2 + xl
    half, yhalf = nz // 2, ny // 2
    n, cap, edge = tiles.shape[0], tiles.shape[1], tiles.shape[2]
    slots = n * cap

    partner = ((1 - xh) * ny + y, rep)
    core_peer = (row, rep + 1 - 2 * c)
    x_peer = (row, z * 4 + (1 - xl) * 2 + c)

    def z_peer(d):
        return (row, lax.rem(z + d + nz, nz) * 4 + xl * 2 + c)

    def y_peer(d):
        return (xh * ny + lax.rem(y + d + ny, ny), rep)

    def x4_peer(d):
        q = lax.rem(x + d, 4)
        return ((q // 2) * ny + y, z * 4 + lax.rem(q, 2) * 2 + c)

    started = []

    def send(src, dst, s_sem, r_sem, peer):
        copy = pltpu.make_async_remote_copy(src, dst, s_sem, r_sem, device_id=peer, device_id_type=MESH)
        copy.start()
        started.append(copy)
        return copy

    load_tiles = pltpu.make_async_copy(tile_ref, tiles, t_s)
    load_tiles.start()
    barrier = pltpu.get_barrier_semaphore()
    peers = [partner, core_peer, x_peer, z_peer(1), y_peer(1)]
    if nz > 2:
        peers.append(z_peer(-1))
    if ny > 2:
        peers.append(y_peer(-1))
    for peer in peers:
        pl.semaphore_signal(barrier, inc=1, device_id=peer, device_id_type=MESH)
    tiles_all = nz * 8
    codes_v[...], ends_v[...] = sort_slots(pos_ref[0], cnt_ref[...], tiles_all, ends_v.shape[1])
    to_scalar = [pltpu.make_async_copy(codes_v, codes, i_s.at[0]), pltpu.make_async_copy(ends_v, ends, i_s.at[1])]
    for copy in to_scalar:
        copy.start()
    load_tiles.wait()
    pl.semaphore_wait(barrier, len(peers))

    flows = [(0, 1, yhalf), (0, -1, yhalf - 1), (1, 1, yhalf - 1), (1, -1, yhalf)]
    last = [[None] * PIECES for _ in range(4)]
    cross = [None] * PIECES
    part = edge * 2 // PIECES
    gather_count = [0]

    def gather_send(src, slot, p, peer):
        k = gather_count[0]
        gather_count[0] += 1
        return send(src, xall.at[slot, p], ag_s.at[k], ag_r.at[k], peer)

    def slot_of(side, shift):
        return side * ny + lax.rem(y + shift + ny, ny)

    def product(slot, ref=None):
        if ref is None:
            both = jnp.concatenate([xall[slot, p] for p in range(PIECES)], axis=1)
        else:
            both = jnp.concatenate([ref[:edge], ref[edge:]], axis=1)

        def some(q, carry):
            out = jnp.dot(
                tiles[slot, pl.ds(q * 4, 4)].reshape(4 * edge, edge), both, preferred_element_type=F32
            )
            at = slot * cap + q * 4
            prod[0, pl.ds(at, 4)] = out[:, :edge].reshape(4, edge, edge)
            prod[1, pl.ds(at, 4)] = out[:, edge:].reshape(4, edge, edge)
            return carry

        lax.fori_loop(0, cap // 4, some, 0)

    g_count = [0]
    near, seen = {}, set()
    sides = (xl, 1 - xl)

    def g_send(src, d, side, x_lo, peer):
        k = g_count[0]
        g_count[0] += 1
        near[d, side] = send(src, gall.at[reach + d, x_lo], g_s.at[k], g_r.at[k], peer)

    def g_wait(d, side):
        if (d, side) not in seen:
            seen.add((d, side))
            near[d, side].wait_recv()

    for step in range(yhalf):
        arrived = []
        for f, (side, way, steps) in enumerate(flows):
            which = xh if side == 0 else 1 - xh
            slot = slot_of(which, -way * step)
            if step > steps:
                continue
            for p in range(PIECES):
                src = xall.at[slot, p]
                if step == 0:
                    if side == 0:
                        src = x_ref.at[pl.ds(p * part, part)]
                    elif cross[p] is not None:
                        cross[p].wait_recv()
                        cross[p] = None
                else:
                    last[f][p].wait_recv()
                if step < steps:
                    last[f][p] = gather_send(src, slot, p, y_peer(way))
                if step == 0 and f == 0:
                    cross[p] = gather_send(src, row, p, partner)
                    if p == PIECES - 1:
                        g_send(g_ref, 0, 1, xl, x_peer)
                        if reach >= 1:
                            for zway in (1, -1):
                                g_send(g_ref, -zway, 0, xl, z_peer(zway))
            if step > 0:
                arrived.append(slot)
        if step == 0:
            for p in range(PIECES):
                if cross[p] is not None:
                    cross[p].wait_recv()
            product(row, x_ref)
            product((1 - xh) * ny + y)
        for slot in arrived:
            product(slot)
        if step == 1 or yhalf == 1:
            if reach >= 1:
                g_wait(0, 1)
                for zway in (1, -1):
                    g_send(gall.at[reach, 1 - xl], -zway, 1, 1 - xl, z_peer(zway))
        if step == 2 or (yhalf <= 2 and step == yhalf - 1):
            for hop in range(1, reach):
                for zway in (1, -1):
                    for side in range(2):
                        g_wait(-zway * hop, side)
                        g_send(
                            gall.at[reach - zway * hop, sides[side]],
                            -zway * (hop + 1), side, sides[side], z_peer(zway),
                        )
    for f, (side, way, steps) in enumerate(flows):
        if steps < yhalf:
            continue
        for p in range(PIECES):
            last[f][p].wait_recv()
        product(slot_of(xh if side == 0 else 1 - xh, -way * yhalf))

    for copy in to_scalar:
        copy.wait()

    def accumulate(k, run):
        code = codes[0, k]
        before = codes[0, jnp.maximum(k - 1, 0)]
        same = lax.div(code, 2 * slots) == lax.div(before, 2 * slots)
        run = prod[lax.rem(code, 2), lax.rem(lax.div(code, 2), slots)] + jnp.where(same, run, 0.0)
        runs[k] = run
        return run

    lax.fori_loop(0, slots, accumulate, jnp.zeros((edge, edge), F32), unroll=2)

    def tile_sum(t):
        upto = ends[0, t]
        below = jnp.where(t > 0, ends[0, jnp.maximum(t - 1, 0)], 0)
        return jnp.where(upto > below, runs[jnp.maximum(upto - 1, 0)], 0.0)

    def at_z(d):
        return lax.rem(z + d + nz, nz)

    order = [half]
    for d in range(half - 1, 0, -1):
        order += [d, -d]
    order.append(0)
    from_core = {}
    for k, d in enumerate(order):
        at = at_z(d)
        for side in range(XL):
            first = ((at * XL + side) * CORES + 1 - c) * 2
            for h in range(2):
                oth[at, side, h * edge : (h + 1) * edge] = tile_sum(first + h).astype(BF16)
        from_core[d] = send(oth.at[at], cbuf.at[at], c_s.at[k], c_r.at[k], core_peer)
    ready = set()

    def mine(d, side):
        if d == -half:
            d = half
        if d not in ready:
            from_core[d].wait_recv()
            ready.add(d)
        at = at_z(d)
        first = ((at * XL + side) * CORES + c) * 2
        own = jnp.concatenate([tile_sum(first), tile_sum(first + 1)], axis=0)
        return own + cbuf[at, side].astype(F32)

    def grad_term(m, g):
        high = m.astype(BF16)
        rest = m - high.astype(F32)
        middle = rest.astype(BF16)
        low = (rest - middle.astype(F32)).astype(BF16)
        total = None
        for v in (high, middle, low):
            term = lax.dot_general(v, g, (((0,), (0,)), ((), ())), preferred_element_type=F32)
            total = term if total is None else total + term
        return total

    def g_of(d, side):
        if (d, side) == (0, 0):
            return g_ref[...]
        g_wait(d, side)
        return gall[reach + d, sides[side]]

    side_a, side_b = 1 - xl, xl
    zflows = [(0, 1, half), (0, -1, half - 1), (1, 1, half - 1), (1, -1, half)]
    zlast = [None] * 4
    count = [0]

    def ring_step(distance, terms=None):
        for f, (side, way, steps) in enumerate(zflows):
            if distance > steps:
                continue
            total = mine(way * distance, side_a if side == 0 else side_b)
            if zlast[f] is not None:
                zlast[f][0].wait_recv()
                total = total + rbuf[zlast[f][1]].astype(F32)
            k = count[0]
            count[0] += 1
            sbuf[k] = total.astype(BF16)
            zlast[f] = (send(sbuf.at[k], rbuf.at[k], z_s.at[k], z_r.at[k], z_peer(way)), k)
            if terms is not None:
                mbuf[terms + f] = total

    def ring_end(side, first, second):
        total = mine(0, side)
        for f in (first, second):
            if zlast[f] is not None:
                zlast[f][0].wait_recv()
                total = total + rbuf[zlast[f][1]].astype(F32)
        return total

    for distance in range(half, reach, -1):
        ring_step(distance)
    if reach >= 1:
        inner = None
        for d in range(1 - reach, reach):
            for s_i, side in ((1, side_a), (0, side_b)):
                term = grad_term(mine(d, side), g_of(d, s_i))
                inner = term if inner is None else inner + term
        gbuf[...] = inner
        ring_step(reach, 0)
        outer = gbuf[...]
        for f, (side, way, steps) in enumerate(zflows):
            outer = outer + grad_term(mbuf[f], g_of(way * reach, 1 if side == 0 else 0))
        gbuf[...] = outer
    else:
        xsend[...] = ring_end(side_a, 0, 1)
        over = send(xsend, xrecv, x_s, x_r, x_peer)
        mbuf[0] = ring_end(side_b, 2, 3)
        gbuf[...] = grad_term(xsend[...], g_of(0, 1)) + grad_term(mbuf[0], g_of(0, 0))

    used = [0]

    def pair():
        k = used[0]
        used[0] += 1
        return a_s.at[k], a_r.at[k]

    def total_of(slots_ref, m):
        total = slots_ref[0]
        for k in range(1, m):
            total = total + slots_ref[k]
        return total

    hrows = gbuf.shape[0] // 2
    here = pl.ds(pl.multiple_of(c * hrows, hrows), hrows)
    there = pl.ds(pl.multiple_of((1 - c) * hrows, hrows), hrows)
    first = send(gbuf.at[there], r1, *pair(), core_peer)
    first.wait_recv()
    hbuf[...] = (gbuf[here] + r1[...]).reshape(hbuf.shape)
    r2[y] = hbuf[y]
    over_y = [send(hbuf.at[lax.rem(y + d, ny)], r2.at[y], *pair(), y_peer(d)) for d in range(1, ny)]
    for distance in range(reach - 1, 0, -1):
        ring_step(distance)
    for copy in over_y:
        copy.wait_recv()
    vbuf[...] = total_of(r2, ny)
    r3[x] = vbuf[...]
    over_x = [send(vbuf, r3.at[x], *pair(), x4_peer(d)) for d in range(1, 4)]
    if reach >= 1:
        xsend[...] = ring_end(side_a, 0, 1)
        over = send(xsend, xrecv, x_s, x_r, x_peer)
        mbuf[0] = ring_end(side_b, 2, 3)
    for copy in over_x:
        copy.wait_recv()
    ubuf[...] = total_of(r3, 4)
    r4[z] = ubuf[...]
    over_z = [send(ubuf, r4.at[z], *pair(), z_peer(d)) for d in range(1, nz)]
    over.wait_recv()
    aggregate = mbuf[0] + xrecv[...]
    mixed_ref[...] = jnp.dot(
        aggregate.astype(BF16), w_ref[...], preferred_element_type=F32
    ).astype(BF16)
    for copy in over_z:
        copy.wait_recv()
    tbuf[...] = total_of(r4, nz)
    r5[y] = tbuf[...]
    back = [send(tbuf, r5.at[y], *pair(), y_peer(d)) for d in range(1, ny)]
    other = [send(tbuf, r6.at[y], *pair(), core_peer)]
    for d, copy in enumerate(back):
        copy.wait_recv()
        at = lax.rem(y - (d + 1) + ny, ny)
        other.append(send(r5.at[at], r6.at[at], *pair(), core_peer))
    for copy in other:
        copy.wait_recv()
    grad_ref[here] = r5[...].reshape(hrows, -1)
    grad_ref[there] = r6[...].reshape(hrows, -1)
    for copy in started:
        copy.wait_send()


def body(node_features, layer_weight, tile_values, tile_positions, section_tile_count, out_cotangent):
    sections, cap, edge, _ = tile_values.shape[1:]
    ny = sections // XH
    nz = lax.axis_size("rep") // (XL * CORES)
    reach = min(2, nz // 2 - 1)
    slots = sections * cap
    f, h = layer_weight.shape
    rows = out_cotangent.shape[0]
    copies = 2 * (nz - 1)
    gathers = PIECES * (1 + 2 * (ny - 1))
    g_copies = 1 + 4 * reach
    hrows = f // 2
    piece = hrows // ny
    small = 1 + 2 * (ny - 1) + 3 + (nz - 1) + ny
    width = max(128, nz * 8)
    dma, vmem, smem = pltpu.SemaphoreType.DMA, pltpu.VMEM, pltpu.SMEM
    whole = pl.BlockSpec(memory_space=pltpu.VMEM)
    return pl.pallas_call(
        functools.partial(kernel, ny, nz, reach),
        out_shape=(
            jax.ShapeDtypeStruct((rows, h), BF16),
            jax.ShapeDtypeStruct((f, h), F32),
        ),
        in_specs=[whole, whole, pl.BlockSpec(memory_space=pl.ANY), whole, whole, whole],
        out_specs=(whole, whole),
        scratch_shapes=[
            vmem((sections, cap, edge, edge), BF16),
            vmem((sections, PIECES, rows // PIECES, f), BF16),
            vmem((2, slots, edge, f), F32),
            vmem((slots, edge, f), F32),
            vmem((1, slots), I32),
            vmem((1, width), I32),
            smem((1, slots), I32),
            smem((1, width), I32),
            vmem((2 * reach + 1, XL, rows, h), BF16),
            vmem((nz, XL, rows, f), BF16),
            vmem((nz, XL, rows, f), BF16),
            vmem((copies, rows, f), BF16),
            vmem((copies, rows, f), BF16),
            vmem((4, rows, f), F32),
            vmem((rows, f), F32),
            vmem((rows, f), F32),
            vmem((f, h), F32),
            vmem((hrows, h), F32),
            vmem((ny, piece, h), F32),
            vmem((ny, piece, h), F32),
            vmem((piece, h), F32),
            vmem((4, piece, h), F32),
            vmem((piece, h), F32),
            vmem((nz, piece, h), F32),
            vmem((piece, h), F32),
            vmem((ny, piece, h), F32),
            vmem((ny, piece, h), F32),
            dma, dma((2,)), dma((gathers,)), dma((gathers,)), dma((g_copies,)), dma((g_copies,)),
            dma((nz,)), dma((nz,)), dma((copies,)), dma((copies,)), dma, dma, dma((small,)), dma((small,)),
        ],
        compiler_params=pltpu.CompilerParams(
            collective_id=0, has_side_effects=True, vmem_limit_bytes=56 << 20
        ),
        name="graph_layer",
    )(node_features, layer_weight, tile_values[0], tile_positions, section_tile_count, out_cotangent)


def solution(mesh):
    placed = (
        P(("row", "rep"), None),
        P(),
        P("row", "rep", None, None, None),
        P("row", "rep", None),
        P("row", "rep"),
        P(("row", "rep"), None),
    )
    return jax.shard_map(
        body, mesh=mesh, in_specs=placed, out_specs=(P(("row", "rep"), None), P()), check_vma=False
    )
```

time: 871 us -> 89.4 us (0.10)
  waiting for transfers between devices: 739 us -> 0 us
  Pallas kernels: 0 us -> 84.1 us
  other arithmetic: 54.3 us -> 0 us
  local copies, waits for them, and re-layouts: 37.7 us -> 4.49 us
  matrix products: 22.3 us -> 0 us
  between operations: 13.8 us -> 0.64 us
    psum x1 -> x0, waiting for transfers between devices: 459 us -> none  [body(): summed_grad = lax.psum(local_grad, ('row', 'rep'))]
    reduce_scatter x1 -> x0, waiting for transfers between devices: 183 us -> none  [body(): lax.psum_scatter(partial_value, 'rep', scatter_dimension=0, tiled=True)]
    all_gather x1 -> x0, waiting for transfers between devices: 96.4 us -> none  [body(): collected_rows = lax.all_gather(node_features, 'row', axis=0, tiled=True)]
    pallas_call x0 -> x1, Pallas kernels: none -> 84.1 us  [body(): pl.pallas_call(functools.partial(kernel, ny, nz, reach), out_shape=(jax.S...]
    scatter-add x16 -> x0, other arithmetic: 43.2 us -> none  [section_add(): return shaped.at[tile_row].add(tile_products).reshape(partial_value.shape)]
    dynamic_slice x32 -> x0, local copies, waits for them, and re-layouts: 22.9 us -> none  [the longest x16 13.6 us: through_all(): lax.dynamic_slice_in_dim(collected_rows, offset * rows_held, rows_held, 0)]
    dot_general x18 -> x0, matrix products: 22.3 us -> none  [the longest x16 18.7 us: section_add(): jnp.einsum('nqi,nir->nqr', adjacency_values, selected_tiles, preferred_el...]
    lt x16 -> x0, other arithmetic: 10.4 us -> none  [section_add(): living = jnp.arange(adjacency_values.shape[0], dtype=jnp.int32) < live_count]
  transfers between devices with their start and end apart: 3 -> 0, of which waited for: 3 -> 0; matrix products, arithmetic and copies ran while one was open for 0% -> 0% of each run, Pallas kernels for 0% -> 0%
where the time goes in v2:
time: 89.4 us; the launch traced here: 89.2 us
  Pallas kernels  84.1 us (94%)
  local copies, waits for them, and re-layouts  4.49 us (5%)
    pallas_call x1, Pallas kernels, body(): pl.pallas_call(functools.partial(kernel, ny, nz, reach), out_shape=(jax.S...  84.1 us
    unnamed x3, local copies, waits for them, and re-layouts  4.49 us

profile of v2, /device:TPU:1, one launch (start us, length us, event | category | flops | bytes accessed | tf_op | source)
XLA Modules:
  0.0 89.2 jit_solution(3724122315441780233)
XLA Ops:
  0.6 1.4 %copy.8.pos_ref = s32[1,16,8]{2,1,0:T(8,128)} copy(s32[1,16,8]{1,2,0:T(8,128)} %param.9) | data formatting | bytes 1024 | tf_op args[3]
  2.0 84.1 %graph_layer.1 = (bf16[256,256]{1,0:T(8,128)(2,1)}, f32[128,256]{1,0:T(8,128)}) custom-call(bf16[256,128]{1,0:T(8,128)(2,1)} %x_ref.1, bf16[128,256]{1,0:T(8,128)(2,1)} %w_ref.1, bf16[16,8,128,128]{3,2,1,0:T(8,128)(2,1)} %bitcast.1, s32[1,16,8]{2,1,0:T(8,128)} %copy.8.pos_ref, s32[1,16]{1,0:T(1,128)} %cnt_ref.1, bf16[256,256]{1,0:T(8,128)(2,1)} %g_ref.1), custom_call_target="tpu_custom_call" | custom-call | tf_op jit(solution)/shard_map/graph_layer/pallas_call | solution.py:385
  86.1 1.6 %copy.11 = bf16[256,256]{1,0:T(8,128)(2,1)} copy(bf16[256,256]{1,0:T(8,128)(2,1)} %get-tuple-element.4) | data formatting | bytes 262144
  87.6 1.6 %copy.12 = f32[128,256]{1,0:T(8,128)} copy(f32[128,256]{1,0:T(8,128)} %get-tuple-element.5) | data formatting | bytes 262144

commit v3 on v2

--- a/solution.py
+++ b/solution.py
@@ -84,17 +84,8 @@
         peers.append(y_peer(-1))
     for peer in peers:
         pl.semaphore_signal(barrier, inc=1, device_id=peer, device_id_type=MESH)
-    tiles_all = nz * 8
-    codes_v[...], ends_v[...] = sort_slots(pos_ref[0], cnt_ref[...], tiles_all, ends_v.shape[1])
-    to_scalar = [pltpu.make_async_copy(codes_v, codes, i_s.at[0]), pltpu.make_async_copy(ends_v, ends, i_s.at[1])]
-    for copy in to_scalar:
-        copy.start()
-    load_tiles.wait()
     pl.semaphore_wait(barrier, len(peers))
 
-    flows = [(0, 1, yhalf), (0, -1, yhalf - 1), (1, 1, yhalf - 1), (1, -1, yhalf)]
-    last = [[None] * PIECES for _ in range(4)]
-    cross = [None] * PIECES
     part = edge * 2 // PIECES
     gather_count = [0]
 
@@ -137,62 +128,88 @@
             seen.add((d, side))
             near[d, side].wait_recv()
 
-    for step in range(yhalf):
-        arrived = []
-        for f, (side, way, steps) in enumerate(flows):
-            which = xh if side == 0 else 1 - xh
-            slot = slot_of(which, -way * step)
-            if step > steps:
-                continue
+    bound = yhalf // 2
+    chains, over = {}, {}
+
+    def steps_of(side, way, p):
+        if side == 1:
+            return bound
+        return yhalf if (way == 1) == (p == 0) else yhalf - 1
+
+    def forward(side, way, p, distance):
+        slot = slot_of(xh if side == 0 else 1 - xh, -way * distance)
+        src = xall.at[slot, p]
+        if distance == 0 and side == 0:
+            src = x_ref.at[pl.ds(p * part, part)]
+        elif distance > 0:
+            chains[side, way, p].wait_recv()
+        if distance < steps_of(side, way, p):
+            chains[side, way, p] = gather_send(src, slot, p, y_peer(way))
+        if side == 0 and distance > bound:
+            over[way, p, distance] = gather_send(src, slot, p, partner)
+
+    def from_partner(distance):
+        for way in (1, -1):
             for p in range(PIECES):
-                src = xall.at[slot, p]
-                if step == 0:
-                    if side == 0:
-                        src = x_ref.at[pl.ds(p * part, part)]
-                    elif cross[p] is not None:
-                        cross[p].wait_recv()
-                        cross[p] = None
-                else:
-                    last[f][p].wait_recv()
-                if step < steps:
-                    last[f][p] = gather_send(src, slot, p, y_peer(way))
-                if step == 0 and f == 0:
-                    cross[p] = gather_send(src, row, p, partner)
-                    if p == PIECES - 1:
-                        g_send(g_ref, 0, 1, xl, x_peer)
-                        if reach >= 1:
-                            for zway in (1, -1):
-                                g_send(g_ref, -zway, 0, xl, z_peer(zway))
-            if step > 0:
-                arrived.append(slot)
-        if step == 0:
+                if distance <= steps_of(0, way, p):
+                    over[way, p, distance].wait_recv()
+        for way in (1, -1) if distance < yhalf else (1,):
+            product(slot_of(1 - xh, -way * distance))
+
+    def send_g(hop):
+        for zway in (1, -1):
+            for side in range(2):
+                g_wait(-zway * hop, side)
+                g_send(
+                    gall.at[reach - zway * hop, sides[side]],
+                    -zway * (hop + 1), side, sides[side], z_peer(zway),
+                )
+
+    for p in range(PIECES):
+        for way in (1, -1):
+            forward(0, way, p, 0)
+        over[0, p, 0] = gather_send(x_ref.at[pl.ds(p * part, part)], row, p, partner)
+    g_send(g_ref, 0, 1, xl, x_peer)
+    if reach >= 1:
+        for zway in (1, -1):
+            g_send(g_ref, -zway, 0, xl, z_peer(zway))
+    tiles_all = nz * 8
+    codes_v[...], ends_v[...] = sort_slots(pos_ref[0], cnt_ref[...], tiles_all, ends_v.shape[1])
+    to_scalar = [pltpu.make_async_copy(codes_v, codes, i_s.at[0]), pltpu.make_async_copy(ends_v, ends, i_s.at[1])]
+    for copy in to_scalar:
+        copy.start()
+    load_tiles.wait()
+    product(row, x_ref)
+    for p in range(PIECES):
+        over[0, p, 0].wait_recv()
+        if bound > 0:
+            for way in (1, -1):
+                forward(1, way, p, 0)
+    product((1 - xh) * ny + y)
+    for distance in range(1, yhalf + 1):
+        for p in range(PIECES):
+            for way in (1, -1):
+                if distance <= steps_of(0, way, p):
+                    forward(0, way, p, distance)
+        if distance <= bound:
             for p in range(PIECES):
-                if cross[p] is not None:
-                    cross[p].wait_recv()
-            product(row, x_ref)
-            product((1 - xh) * ny + y)
-        for slot in arrived:
-            product(slot)
-        if step == 1 or yhalf == 1:
-            if reach >= 1:
-                g_wait(0, 1)
-                for zway in (1, -1):
-                    g_send(gall.at[reach, 1 - xl], -zway, 1, 1 - xl, z_peer(zway))
-        if step == 2 or (yhalf <= 2 and step == yhalf - 1):
-            for hop in range(1, reach):
-                for zway in (1, -1):
-                    for side in range(2):
-                        g_wait(-zway * hop, side)
-                        g_send(
-                            gall.at[reach - zway * hop, sides[side]],
-                            -zway * (hop + 1), side, sides[side], z_peer(zway),
-                        )
-    for f, (side, way, steps) in enumerate(flows):
-        if steps < yhalf:
-            continue
-        for p in range(PIECES):
-            last[f][p].wait_recv()
-        product(slot_of(xh if side == 0 else 1 - xh, -way * yhalf))
+                for way in (1, -1):
+                    forward(1, way, p, distance)
+        for way in (1, -1) if distance < yhalf else (1,):
+            product(slot_of(xh, -way * distance))
+        if distance <= bound:
+            for way in (1, -1):
+                product(slot_of(1 - xh, -way * distance))
+        if distance - 1 > bound:
+            from_partner(distance - 1)
+        if distance == 1 and reach >= 1:
+            g_wait(0, 1)
+            for zway in (1, -1):
+                g_send(gall.at[reach, 1 - xl], -zway, 1, 1 - xl, z_peer(zway))
+        for hop in range(1, reach):
+            if distance == min(hop + 1, yhalf):
+                send_g(hop)
+    from_partner(yhalf)
 
     for copy in to_scalar:
         copy.wait()
@@ -219,34 +236,41 @@
     for d in range(half - 1, 0, -1):
         order += [d, -d]
     order.append(0)
-    from_core = {}
-    for k, d in enumerate(order):
+    from_core, ready = {}, set()
+
+    def emit(d):
         at = at_z(d)
         for side in range(XL):
             first = ((at * XL + side) * CORES + 1 - c) * 2
             for h in range(2):
-                oth[at, side, h * edge : (h + 1) * edge] = tile_sum(first + h).astype(BF16)
+                oth[at, side, h] = tile_sum(first + h).astype(BF16)
+        k = len(from_core)
         from_core[d] = send(oth.at[at], cbuf.at[at], c_s.at[k], c_r.at[k], core_peer)
-    ready = set()
-
-    def mine(d, side):
+
+    pending = list(order)
+
+    def emit_some(m):
+        for _ in range(m):
+            if pending:
+                emit(pending.pop(0))
+
+    def mine(d, side, h):
         if d == -half:
             d = half
         if d not in ready:
             from_core[d].wait_recv()
             ready.add(d)
         at = at_z(d)
-        first = ((at * XL + side) * CORES + c) * 2
-        own = jnp.concatenate([tile_sum(first), tile_sum(first + 1)], axis=0)
-        return own + cbuf[at, side].astype(F32)
+        return tile_sum(((at * XL + side) * CORES + c) * 2 + h) + cbuf[at, side, h].astype(F32)
+
+    def mine_both(d, side):
+        return jnp.concatenate([mine(d, side, 0), mine(d, side, 1)], axis=0)
 
     def grad_term(m, g):
         high = m.astype(BF16)
-        rest = m - high.astype(F32)
-        middle = rest.astype(BF16)
-        low = (rest - middle.astype(F32)).astype(BF16)
+        low = (m - high.astype(F32)).astype(BF16)
         total = None
-        for v in (high, middle, low):
+        for v in (high, low):
             term = lax.dot_general(v, g, (((0,), (0,)), ((), ())), preferred_element_type=F32)
             total = term if total is None else total + term
         return total
@@ -259,51 +283,59 @@
 
     side_a, side_b = 1 - xl, xl
     zflows = [(0, 1, half), (0, -1, half - 1), (1, 1, half - 1), (1, -1, half)]
-    zlast = [None] * 4
+    zlast = {}
     count = [0]
 
-    def ring_step(distance, terms=None):
+    def ring_step(distance, terms=False):
         for f, (side, way, steps) in enumerate(zflows):
             if distance > steps:
                 continue
-            total = mine(way * distance, side_a if side == 0 else side_b)
-            if zlast[f] is not None:
-                zlast[f][0].wait_recv()
-                total = total + rbuf[zlast[f][1]].astype(F32)
-            k = count[0]
-            count[0] += 1
-            sbuf[k] = total.astype(BF16)
-            zlast[f] = (send(sbuf.at[k], rbuf.at[k], z_s.at[k], z_r.at[k], z_peer(way)), k)
-            if terms is not None:
-                mbuf[terms + f] = total
-
-    def ring_end(side, first, second):
-        total = mine(0, side)
-        for f in (first, second):
-            if zlast[f] is not None:
-                zlast[f][0].wait_recv()
-                total = total + rbuf[zlast[f][1]].astype(F32)
-        return total
-
+            for h in range(2):
+                total = mine(way * distance, side_a if side == 0 else side_b, h)
+                if (f, h) in zlast:
+                    zlast[f, h][0].wait_recv()
+                    total = total + rbuf[zlast[f, h][1]].astype(F32)
+                k = count[0]
+                count[0] += 1
+                sbuf[k] = total.astype(BF16)
+                zlast[f, h] = (send(sbuf.at[k], rbuf.at[k], z_s.at[k], z_r.at[k], z_peer(way)), k)
+                if terms:
+                    mbuf[h * edge : (h + 1) * edge] = total
+            if terms:
+                gbuf[...] += grad_term(mbuf[...], g_of(way * reach, 1 if side == 0 else 0))
+
+    def ring_end(side, first, second, out):
+        for h in range(2):
+            total = mine(0, side, h)
+            for f in (first, second):
+                if (f, h) in zlast:
+                    zlast[f, h][0].wait_recv()
+                    total = total + rbuf[zlast[f, h][1]].astype(F32)
+            out[h * edge : (h + 1) * edge] = total
+
+    def inner_terms(distances):
+        for d in distances:
+            gbuf[...] += grad_term(mine_both(d, side_a), g_of(d, 1))
+            gbuf[...] += grad_term(mine_both(d, side_b), g_of(d, 0))
+
+    gbuf[...] = jnp.zeros_like(gbuf)
+    inner = sorted(range(1 - reach, reach), key=abs, reverse=True)
+    emit_some(3)
     for distance in range(half, reach, -1):
         ring_step(distance)
+        emit_some(len(pending) if distance <= reach + 2 else 4)
+        if distance == reach + 2:
+            inner_terms(inner[: reach - 1])
+            inner = inner[reach - 1 :]
+    emit_some(len(pending))
     if reach >= 1:
-        inner = None
-        for d in range(1 - reach, reach):
-            for s_i, side in ((1, side_a), (0, side_b)):
-                term = grad_term(mine(d, side), g_of(d, s_i))
-                inner = term if inner is None else inner + term
-        gbuf[...] = inner
-        ring_step(reach, 0)
-        outer = gbuf[...]
-        for f, (side, way, steps) in enumerate(zflows):
-            outer = outer + grad_term(mbuf[f], g_of(way * reach, 1 if side == 0 else 0))
-        gbuf[...] = outer
+        inner_terms(inner)
+        ring_step(reach, True)
     else:
-        xsend[...] = ring_end(side_a, 0, 1)
-        over = send(xsend, xrecv, x_s, x_r, x_peer)
-        mbuf[0] = ring_end(side_b, 2, 3)
-        gbuf[...] = grad_term(xsend[...], g_of(0, 1)) + grad_term(mbuf[0], g_of(0, 0))
+        ring_end(side_a, 0, 1, xsend)
+        over_x_pair = send(xsend, xrecv, x_s, x_r, x_peer)
+        ring_end(side_b, 2, 3, mbuf)
+        gbuf[...] = grad_term(xsend[...], g_of(0, 1)) + grad_term(mbuf[...], g_of(0, 0))
 
     used = [0]
 
@@ -334,16 +366,16 @@
     r3[x] = vbuf[...]
     over_x = [send(vbuf, r3.at[x], *pair(), x4_peer(d)) for d in range(1, 4)]
     if reach >= 1:
-        xsend[...] = ring_end(side_a, 0, 1)
-        over = send(xsend, xrecv, x_s, x_r, x_peer)
-        mbuf[0] = ring_end(side_b, 2, 3)
+        ring_end(side_a, 0, 1, xsend)
+        over_x_pair = send(xsend, xrecv, x_s, x_r, x_peer)
+        ring_end(side_b, 2, 3, mbuf)
     for copy in over_x:
         copy.wait_recv()
     ubuf[...] = total_of(r3, 4)
     r4[z] = ubuf[...]
     over_z = [send(ubuf, r4.at[z], *pair(), z_peer(d)) for d in range(1, nz)]
-    over.wait_recv()
-    aggregate = mbuf[0] + xrecv[...]
+    over_x_pair.wait_recv()
+    aggregate = mbuf[...] + xrecv[...]
     mixed_ref[...] = jnp.dot(
         aggregate.astype(BF16), w_ref[...], preferred_element_type=F32
     ).astype(BF16)
@@ -369,11 +401,11 @@
     sections, cap, edge, _ = tile_values.shape[1:]
     ny = sections // XH
     nz = lax.axis_size("rep") // (XL * CORES)
-    reach = min(2, nz // 2 - 1)
+    reach = min(3, nz // 2 - 1)
     slots = sections * cap
     f, h = layer_weight.shape
     rows = out_cotangent.shape[0]
-    copies = 2 * (nz - 1)
+    copies = 4 * (nz - 1)
     gathers = PIECES * (1 + 2 * (ny - 1))
     g_copies = 1 + 4 * reach
     hrows = f // 2
@@ -400,11 +432,11 @@
             smem((1, slots), I32),
             smem((1, width), I32),
             vmem((2 * reach + 1, XL, rows, h), BF16),
-            vmem((nz, XL, rows, f), BF16),
-            vmem((nz, XL, rows, f), BF16),
-            vmem((copies, rows, f), BF16),
-            vmem((copies, rows, f), BF16),
-            vmem((4, rows, f), F32),
+            vmem((nz, XL, 2, edge, f), BF16),
+            vmem((nz, XL, 2, edge, f), BF16),
+            vmem((copies, edge, f), BF16),
+            vmem((copies, edge, f), BF16),
+            vmem((rows, f), F32),
             vmem((rows, f), F32),
             vmem((rows, f), F32),
             vmem((f, h), F32),

time: 89.4 us -> 95.2 us (1.065)
  Pallas kernels: 84.1 us -> 89.9 us
    pallas_call x1, Pallas kernels: 84.1 us -> 89.9 us  [body(): pl.pallas_call(functools.partial(kernel, ny, nz, reach), out_shape=(jax.S...]
where the time goes in v3:
time: 95.2 us; the launch traced here: 95 us
  Pallas kernels  89.9 us (94%)
  local copies, waits for them, and re-layouts  4.49 us (5%)
    pallas_call x1, Pallas kernels, body(): pl.pallas_call(functools.partial(kernel, ny, nz, reach), out_shape=(jax.S...  89.9 us
    unnamed x3, local copies, waits for them, and re-layouts  4.49 us

profile of v3, /device:TPU:1, one launch (start us, length us, event | category | flops | bytes accessed | tf_op | source)
XLA Modules:
  0.0 95.0 jit_solution(8018171707528380958)
XLA Ops:
  0.6 1.4 %copy.8.pos_ref = s32[1,16,8]{2,1,0:T(8,128)} copy(s32[1,16,8]{1,2,0:T(8,128)} %param.9) | data formatting | bytes 1024 | tf_op args[3]
  2.0 89.9 %graph_layer.1 = (bf16[256,256]{1,0:T(8,128)(2,1)}, f32[128,256]{1,0:T(8,128)}) custom-call(bf16[256,128]{1,0:T(8,128)(2,1)} %x_ref.1, bf16[128,256]{1,0:T(8,128)(2,1)} %w_ref.1, bf16[16,8,128,128]{3,2,1,0:T(8,128)(2,1)} %bitcast.1, s32[1,16,8]{2,1,0:T(8,128)} %copy.8.pos_ref, s32[1,16]{1,0:T(1,128)} %cnt_ref.1, bf16[256,256]{1,0:T(8,128)(2,1)} %g_ref.1), custom_call_target="tpu_custom_call" | custom-call | tf_op jit(solution)/shard_map/graph_layer/pallas_call | solution.py:417
  91.9 1.6 %copy.11 = bf16[256,256]{1,0:T(8,128)(2,1)} copy(bf16[256,256]{1,0:T(8,128)(2,1)} %get-tuple-element.4) | data formatting | bytes 262144
  93.4 1.6 %copy.12 = f32[128,256]{1,0:T(8,128)} copy(f32[128,256]{1,0:T(8,128)} %get-tuple-element.5) | data formatting | bytes 262144

commit v4 on v3

--- a/solution.py
+++ b/solution.py
@@ -84,6 +84,11 @@
         peers.append(y_peer(-1))
     for peer in peers:
         pl.semaphore_signal(barrier, inc=1, device_id=peer, device_id_type=MESH)
+    tiles_all = nz * 8
+    codes_v[...], ends_v[...] = sort_slots(pos_ref[0], cnt_ref[...], tiles_all, ends_v.shape[1])
+    to_scalar = [pltpu.make_async_copy(codes_v, codes, i_s.at[0]), pltpu.make_async_copy(ends_v, ends, i_s.at[1])]
+    for copy in to_scalar:
+        copy.start()
     pl.semaphore_wait(barrier, len(peers))
 
     part = edge * 2 // PIECES
@@ -128,13 +133,10 @@
             seen.add((d, side))
             near[d, side].wait_recv()
 
-    bound = yhalf // 2
     chains, over = {}, {}
 
     def steps_of(side, way, p):
-        if side == 1:
-            return bound
-        return yhalf if (way == 1) == (p == 0) else yhalf - 1
+        return yhalf if ((way == 1) == (p == 0)) == (side == 0) else yhalf - 1
 
     def forward(side, way, p, distance):
         slot = slot_of(xh if side == 0 else 1 - xh, -way * distance)
@@ -145,16 +147,6 @@
             chains[side, way, p].wait_recv()
         if distance < steps_of(side, way, p):
             chains[side, way, p] = gather_send(src, slot, p, y_peer(way))
-        if side == 0 and distance > bound:
-            over[way, p, distance] = gather_send(src, slot, p, partner)
-
-    def from_partner(distance):
-        for way in (1, -1):
-            for p in range(PIECES):
-                if distance <= steps_of(0, way, p):
-                    over[way, p, distance].wait_recv()
-        for way in (1, -1) if distance < yhalf else (1,):
-            product(slot_of(1 - xh, -way * distance))
 
     def send_g(hop):
         for zway in (1, -1):
@@ -168,48 +160,34 @@
     for p in range(PIECES):
         for way in (1, -1):
             forward(0, way, p, 0)
-        over[0, p, 0] = gather_send(x_ref.at[pl.ds(p * part, part)], row, p, partner)
+        over[p] = gather_send(x_ref.at[pl.ds(p * part, part)], row, p, partner)
     g_send(g_ref, 0, 1, xl, x_peer)
     if reach >= 1:
         for zway in (1, -1):
             g_send(g_ref, -zway, 0, xl, z_peer(zway))
-    tiles_all = nz * 8
-    codes_v[...], ends_v[...] = sort_slots(pos_ref[0], cnt_ref[...], tiles_all, ends_v.shape[1])
-    to_scalar = [pltpu.make_async_copy(codes_v, codes, i_s.at[0]), pltpu.make_async_copy(ends_v, ends, i_s.at[1])]
-    for copy in to_scalar:
-        copy.start()
+    for p in range(PIECES):
+        over[p].wait_recv()
+        for way in (1, -1):
+            forward(1, way, p, 0)
     load_tiles.wait()
     product(row, x_ref)
-    for p in range(PIECES):
-        over[0, p, 0].wait_recv()
-        if bound > 0:
-            for way in (1, -1):
-                forward(1, way, p, 0)
     product((1 - xh) * ny + y)
     for distance in range(1, yhalf + 1):
-        for p in range(PIECES):
-            for way in (1, -1):
-                if distance <= steps_of(0, way, p):
-                    forward(0, way, p, distance)
-        if distance <= bound:
+        ways = (1, -1) if distance < yhalf else (1,)
+        for side in range(2):
             for p in range(PIECES):
                 for way in (1, -1):
-                    forward(1, way, p, distance)
-        for way in (1, -1) if distance < yhalf else (1,):
-            product(slot_of(xh, -way * distance))
-        if distance <= bound:
-            for way in (1, -1):
-                product(slot_of(1 - xh, -way * distance))
-        if distance - 1 > bound:
-            from_partner(distance - 1)
+                    if distance <= steps_of(side, way, p):
+                        forward(side, way, p, distance)
+        for side in range(2):
+            for way in ways:
+                product(slot_of(xh if side == 0 else 1 - xh, -way * distance))
         if distance == 1 and reach >= 1:
             g_wait(0, 1)
             for zway in (1, -1):
                 g_send(gall.at[reach, 1 - xl], -zway, 1, 1 - xl, z_peer(zway))
-        for hop in range(1, reach):
-            if distance == min(hop + 1, yhalf):
-                send_g(hop)
-    from_partner(yhalf)
+    for hop in range(1, reach):
+        send_g(hop)
 
     for copy in to_scalar:
         copy.wait()
@@ -339,6 +317,9 @@
 
     used = [0]
 
+    def farthest_first(m):
+        return sorted(range(1, m), key=lambda d: -min(d, m - d))
+
     def pair():
         k = used[0]
         used[0] += 1
@@ -357,14 +338,14 @@
     first.wait_recv()
     hbuf[...] = (gbuf[here] + r1[...]).reshape(hbuf.shape)
     r2[y] = hbuf[y]
-    over_y = [send(hbuf.at[lax.rem(y + d, ny)], r2.at[y], *pair(), y_peer(d)) for d in range(1, ny)]
+    over_y = [send(hbuf.at[lax.rem(y + d, ny)], r2.at[y], *pair(), y_peer(d)) for d in farthest_first(ny)]
     for distance in range(reach - 1, 0, -1):
         ring_step(distance)
     for copy in over_y:
         copy.wait_recv()
     vbuf[...] = total_of(r2, ny)
     r3[x] = vbuf[...]
-    over_x = [send(vbuf, r3.at[x], *pair(), x4_peer(d)) for d in range(1, 4)]
+    over_x = [send(vbuf, r3.at[x], *pair(), x4_peer(d)) for d in farthest_first(4)]
     if reach >= 1:
         ring_end(side_a, 0, 1, xsend)
         over_x_pair = send(xsend, xrecv, x_s, x_r, x_peer)
@@ -373,7 +354,7 @@
         copy.wait_recv()
     ubuf[...] = total_of(r3, 4)
     r4[z] = ubuf[...]
-    over_z = [send(ubuf, r4.at[z], *pair(), z_peer(d)) for d in range(1, nz)]
+    over_z = [send(ubuf, r4.at[z], *pair(), z_peer(d)) for d in farthest_first(nz)]
     over_x_pair.wait_recv()
     aggregate = mbuf[...] + xrecv[...]
     mixed_ref[...] = jnp.dot(
@@ -383,11 +364,11 @@
         copy.wait_recv()
     tbuf[...] = total_of(r4, nz)
     r5[y] = tbuf[...]
-    back = [send(tbuf, r5.at[y], *pair(), y_peer(d)) for d in range(1, ny)]
+    back = {d: send(tbuf, r5.at[y], *pair(), y_peer(d)) for d in farthest_first(ny)}
     other = [send(tbuf, r6.at[y], *pair(), core_peer)]
-    for d, copy in enumerate(back):
-        copy.wait_recv()
-        at = lax.rem(y - (d + 1) + ny, ny)
+    for d in reversed(farthest_first(ny)):
+        back[d].wait_recv()
+        at = lax.rem(y - d + ny, ny)
         other.append(send(r5.at[at], r6.at[at], *pair(), core_peer))
     for copy in other:
         copy.wait_recv()
@@ -401,7 +382,7 @@
     sections, cap, edge, _ = tile_values.shape[1:]
     ny = sections // XH
     nz = lax.axis_size("rep") // (XL * CORES)
-    reach = min(3, nz // 2 - 1)
+    reach = min(2, nz // 2 - 1)
     slots = sections * cap
     f, h = layer_weight.shape
     rows = out_cotangent.shape[0]

time: 95.2 us -> 86.3 us (0.907)
  Pallas kernels: 89.9 us -> 80.9 us
    pallas_call x1, Pallas kernels: 89.9 us -> 80.9 us  [body(): pl.pallas_call(functools.partial(kernel, ny, nz, reach), out_shape=(jax.S...]
where the time goes in v4:
time: 86.3 us; the launch traced here: 86.1 us
  Pallas kernels  80.9 us (94%)
  local copies, waits for them, and re-layouts  4.49 us (5%)
    pallas_call x1, Pallas kernels, body(): pl.pallas_call(functools.partial(kernel, ny, nz, reach), out_shape=(jax.S...  80.9 us
    unnamed x3, local copies, waits for them, and re-layouts  4.49 us

profile of v4, /device:TPU:1, one launch (start us, length us, event | category | flops | bytes accessed | tf_op | source)
XLA Modules:
  0.0 86.1 jit_solution(2928749575039678181)
XLA Ops:
  0.6 1.4 %copy.8.pos_ref = s32[1,16,8]{2,1,0:T(8,128)} copy(s32[1,16,8]{1,2,0:T(8,128)} %param.9) | data formatting | bytes 1024 | tf_op args[3]
  2.0 80.9 %graph_layer.1 = (bf16[256,256]{1,0:T(8,128)(2,1)}, f32[128,256]{1,0:T(8,128)}) custom-call(bf16[256,128]{1,0:T(8,128)(2,1)} %x_ref.1, bf16[128,256]{1,0:T(8,128)(2,1)} %w_ref.1, bf16[16,8,128,128]{3,2,1,0:T(8,128)(2,1)} %bitcast.1, s32[1,16,8]{2,1,0:T(8,128)} %copy.8.pos_ref, s32[1,16]{1,0:T(1,128)} %cnt_ref.1, bf16[256,256]{1,0:T(8,128)(2,1)} %g_ref.1), custom_call_target="tpu_custom_call" | custom-call | tf_op jit(solution)/shard_map/graph_layer/pallas_call | solution.py:398
  82.9 1.6 %copy.11 = bf16[256,256]{1,0:T(8,128)(2,1)} copy(bf16[256,256]{1,0:T(8,128)(2,1)} %get-tuple-element.4) | data formatting | bytes 262144
  84.5 1.6 %copy.12 = f32[128,256]{1,0:T(8,128)} copy(f32[128,256]{1,0:T(8,128)} %get-tuple-element.5) | data formatting | bytes 262144

commit v5 on v4

--- a/solution.py
+++ b/solution.py
@@ -18,15 +18,13 @@
 
 
 def sort_slots(pos, cnt, tiles_all, width):
-    n, cap = pos.shape
+    cap, n = pos.shape
     slots = n * cap
-    diag = iota((n, n), 0) == iota((n, n), 1)
-    count = jnp.sum(jnp.where(diag, jnp.broadcast_to(cnt, (n, n)), 0), axis=1, keepdims=True)
-    slot = iota((n, cap), 1)
-    key = jnp.where(slot < count, lax.div(pos, 2), tiles_all)
-    code = (key * slots + iota((n, cap), 0) * cap + slot) * 2 + lax.rem(pos, 2)
-    spread = jnp.broadcast_to(code[:, None, :], (n, cap, cap))
-    picked = jnp.where(iota((n, cap, cap), 1) == iota((n, cap, cap), 2), spread, 0)
+    slot = iota((cap, n), 0)
+    key = jnp.where(slot < cnt, lax.div(pos, 2), tiles_all)
+    code = (key * slots + iota((cap, n), 1) * cap + slot) * 2 + lax.rem(pos, 2)
+    spread = jnp.broadcast_to(code[None, :, :], (n, cap, n))
+    picked = jnp.where(iota((n, cap, n), 0) == iota((n, cap, n), 2), spread, 0)
     column = jnp.sum(picked, axis=2, keepdims=True).reshape(slots, 1)
     grid = jnp.broadcast_to(column, (slots, slots))
     lane = iota((slots, slots), 1)
@@ -182,7 +180,7 @@
         for side in range(2):
             for way in ways:
                 product(slot_of(xh if side == 0 else 1 - xh, -way * distance))
-        if distance == 1 and reach >= 1:
+        if distance == min(2, yhalf) and reach >= 1:
             g_wait(0, 1)
             for zway in (1, -1):
                 g_send(gall.at[reach, 1 - xl], -zway, 1, 1 - xl, z_peer(zway))
@@ -395,6 +393,7 @@
     width = max(128, nz * 8)
     dma, vmem, smem = pltpu.SemaphoreType.DMA, pltpu.VMEM, pltpu.SMEM
     whole = pl.BlockSpec(memory_space=pltpu.VMEM)
+    positions = jnp.swapaxes(tile_positions, 1, 2)
     return pl.pallas_call(
         functools.partial(kernel, ny, nz, reach),
         out_shape=(
@@ -438,7 +437,7 @@
             collective_id=0, has_side_effects=True, vmem_limit_bytes=56 << 20
         ),
         name="graph_layer",
-    )(node_features, layer_weight, tile_values[0], tile_positions, section_tile_count, out_cotangent)
+    )(node_features, layer_weight, tile_values[0], positions, section_tile_count, out_cotangent)
 
 
 def solution(mesh):

time: 86.3 us -> 84.8 us (0.983)
  local copies, waits for them, and re-layouts: 4.49 us -> 3.14 us
    unnamed x3 -> x2, local copies, waits for them, and re-layouts: 4.49 us -> 3.14 us
where the time goes in v5:
time: 84.8 us; the launch traced here: 84.7 us
  Pallas kernels  80.9 us (95%)
  local copies, waits for them, and re-layouts  3.14 us (4%)
    pallas_call x1, Pallas kernels, body(): pl.pallas_call(functools.partial(kernel, ny, nz, reach), out_shape=(jax.S...  80.9 us
    unnamed x2, local copies, waits for them, and re-layouts  3.14 us

profile of v5, /device:TPU:1, one launch (start us, length us, event | category | flops | bytes accessed | tf_op | source)
XLA Modules:
  0.0 84.7 jit_solution(10080100193290035442)
XLA Ops:
  0.6 80.9 %graph_layer.1 = (bf16[256,256]{1,0:T(8,128)(2,1)}, f32[128,256]{1,0:T(8,128)}) custom-call(bf16[256,128]{1,0:T(8,128)(2,1)} %x_ref.1, bf16[128,256]{1,0:T(8,128)(2,1)} %w_ref.1, bf16[16,8,128,128]{3,2,1,0:T(8,128)(2,1)} %bitcast.2, s32[1,8,16]{2,1,0:T(8,128)} %bitcast.3, s32[1,16]{1,0:T(1,128)} %cnt_ref.1, bf16[256,256]{1,0:T(8,128)(2,1)} %g_ref.1), custom_call_target="tpu_custom_call" | custom-call | tf_op jit(solution)/shard_map/graph_layer/pallas_call | solution.py:397
  81.5 1.6 %copy.10 = bf16[256,256]{1,0:T(8,128)(2,1)} copy(bf16[256,256]{1,0:T(8,128)(2,1)} %get-tuple-element.4) | data formatting | bytes 262144
  83.1 1.6 %copy.11 = f32[128,256]{1,0:T(8,128)} copy(f32[128,256]{1,0:T(8,128)} %get-tuple-element.5) | data formatting | bytes 262144
